TPU v7x, 32 devices: a whole 2x2x4 slice. The times are simulated.
32 devices in a mesh: member: 8 (over z, core), state: 4 (over y, x).
Axes of the slice: x: 2, y: 2, z: 4, core: 2. Of those that a mesh axis runs over, the one named last changes fastest.
Arguments:
- prior_analyses: float32 [64, 256, 1024], P('member', 'state'), may hold values from -6 to 6
- smoothing_number: float32 [256, 1024], P('state'), may hold values from 0.08 to 0.24
- observations: float32 [3072], replicated, may hold values from -6 to 6
- obs_variance: float32 [3072], replicated, may hold values from 0.25 to 2
- obs_row: int32 [3072], replicated, may hold values from 0 to 255
- obs_col: int32 [3072], replicated, may hold values from 0 to 1023
- obs_radius: int32 [3072], replicated, may hold values from 32 to 127
- block_order: int32 [3072], replicated, may hold values from 0 to 3071, each once
Outputs:
- analysis: float32 [64, 256, 1024], P('member', 'state')
Inputs may be any that keep to these rules, and one draw needn't show every extreme that they name: `block_order`: every observation index appears exactly once.
All inputs are finite; a program needn't handle non-finite values.
Results may differ from a plain program's by a relative error of at most 0.0035.
Values sent between devices are 32-bit elements; how exact they have to be, the bound alone decides.
A program may use at most 64 MiB of HBM per device.

v0:
```python
import jax
import jax.numpy as jnp
from jax import lax
from jax.sharding import PartitionSpec as P

BLK = 512
NBLK = 6
spread_eps = 1e-06


def extended(shard, sides, width):
    for axis, dim in sides:
        peers, length = (lax.axis_size(axis), shard.shape[dim])
        up = [(i, (i + 1) % peers) for i in range(peers - 1)]
        down = [(j, i) for i, j in up]
        last = lax.slice_in_dim(shard, length - width, length, axis=dim)
        leading = lax.slice_in_dim(shard, 0, width, axis=dim)
        before = lax.ppermute(last, axis, up)
        after = lax.ppermute(leading, axis, down)
        shard = jnp.concatenate([before, shard, after], axis=dim)
    return shard


def advance(padded, spreading_coefficients):
    center = padded[:, 1:-1, :]
    vertical = padded[:, 2:, :] + padded[:, :-2, :]
    sideways = jnp.pad(center[:, :, 1:], ((0, 0), (0, 0), (0, 1))) + jnp.pad(
        center[:, :, :-1], ((0, 0), (0, 0), (1, 0))
    )
    return center + spreading_coefficients * (vertical + sideways - 4.0 * center)


def predicted_level(realization_vectors, spreading_coefficients):
    current = realization_vectors
    for step_index in range(2):
        padded = extended(current, (("state", 1),), 1)
        current = advance(padded, spreading_coefficients)
    return current


def increments(prior_values, value_array, variances):
    realization_vectors = prior_values.shape[0]
    prior_mean = jnp.mean(prior_values, axis=0)
    anomaly = prior_values - prior_mean
    spread = jnp.sum(anomaly * anomaly, axis=0) / (realization_vectors - 1) + spread_eps
    post_var = spread * variances / (spread + variances)
    posterior_average = post_var * (prior_mean / spread + value_array / variances)
    shrink = jnp.sqrt(variances / (variances + spread)) - 1.0
    increment = (posterior_average - prior_mean + shrink * anomaly).astype(jnp.bfloat16)
    return (anomaly.astype(jnp.bfloat16), increment, 1.0 / spread)


def taper_weight(cell_row, cell_col, obs_rows, obs_cols, radius):
    row_gap = cell_row[None, :] - obs_rows[:, None]
    col_gap = cell_col[None, :] - obs_cols[:, None]
    distance = (row_gap * row_gap + col_gap * col_gap).astype(jnp.float32)
    reach = radius.astype(jnp.float32)
    closeness = jnp.maximum(1.0 - distance / (reach * reach)[:, None], 0.0)
    return closeness * closeness


def linear_gain_fit(
    target, target_rows, target_cols, anomaly, increment, inverse, obs_rows, obs_cols, radius
):
    realization_vectors = target.shape[0]
    cell_mean = jnp.mean(target, axis=0)
    cell_anomaly = (target - cell_mean).astype(jnp.bfloat16)
    sub_size = min(anomaly.shape[1], 128)
    accumulated = jnp.zeros(target.shape, jnp.float32)
    for part_index in range(anomaly.shape[1] // sub_size):
        lower_end = part_index * sub_size
        upper_end = lower_end + sub_size
        covariance = lax.dot_general(
            anomaly[:, lower_end:upper_end],
            cell_anomaly,
            (((0,), (0,)), ((), ())),
            preferred_element_type=jnp.float32,
        ) / (realization_vectors - 1)
        weight = taper_weight(
            target_rows,
            target_cols,
            obs_rows[lower_end:upper_end],
            obs_cols[lower_end:upper_end],
            radius[lower_end:upper_end],
        )
        gain_tile = (weight * covariance * inverse[lower_end:upper_end, None]).astype(jnp.bfloat16)
        accumulated = accumulated + jnp.dot(
            increment[:, lower_end:upper_end], gain_tile, preferred_element_type=jnp.float32
        )
    return accumulated


def pick_values(cell_values, rows_wanted, cols_wanted, first_row, tile_rows, tile_cols):
    local_row = rows_wanted - first_row
    inside = (
        (local_row >= 0) & (local_row < tile_rows) & (cols_wanted >= 0) & (cols_wanted < tile_cols)
    )
    local_index = jnp.where(inside, local_row * tile_cols + cols_wanted, 0)
    return jnp.where(inside[None, :], jnp.take(cell_values, local_index, axis=1), 0.0)


def on_device(
    prior_analyses,
    smoothing_number,
    observations,
    obs_variance,
    obs_row,
    obs_col,
    obs_radius,
    block_order,
):
    realization_vectors = predicted_level(prior_analyses, smoothing_number)
    row_count = realization_vectors.shape[1]
    col_count = realization_vectors.shape[2]
    member_count = lax.axis_size("member")
    base_row = lax.axis_index("state") * row_count
    tile_data = lax.all_to_all(
        realization_vectors, "member", split_axis=1, concat_axis=0, tiled=True
    )
    tile_rows = row_count // member_count
    first_row = base_row + lax.axis_index("member") * tile_rows
    grid_point_total = tile_rows * col_count
    cell_values = tile_data.reshape(tile_data.shape[0], grid_point_total)
    position = jnp.arange(grid_point_total, dtype=jnp.int32)
    cell_row = first_row + position // col_count
    cell_col = position % col_count
    for block_index in range(NBLK):
        chosen = block_order[block_index * BLK : (block_index + 1) * BLK]
        block_rows = jnp.take(obs_row, chosen)
        block_cols = jnp.take(obs_col, chosen)
        block_radius = jnp.take(obs_radius, chosen)
        local_values = pick_values(
            cell_values, block_rows, block_cols, first_row, tile_rows, col_count
        )
        prior_values = lax.psum(local_values, ("member", "state"))
        anomaly, increment, inverse = increments(
            prior_values, jnp.take(observations, chosen), jnp.take(obs_variance, chosen)
        )
        cell_values = cell_values + linear_gain_fit(
            cell_values,
            cell_row,
            cell_col,
            anomaly,
            increment,
            inverse,
            block_rows,
            block_cols,
            block_radius,
        )
    result = cell_values.reshape(tile_data.shape)
    return lax.all_to_all(result, "member", split_axis=0, concat_axis=1, tiled=True)


def solution(mesh):
    in_specs = (P("member", "state", None), P("state", None), P(), P(), P(), P(), P(), P())
    out_specs = P("member", "state", None)
    return jax.shard_map(
        on_device, mesh=mesh, in_specs=in_specs, out_specs=out_specs, check_vma=False
    )
```

profile of v0, /device:TPU:0, one launch (start us, length us, event | category | flops | bytes accessed | tf_op | source)
XLA Modules:
  0.0 1187.5 jit_solution(11396176168441743626)
XLA Ops:
  9.4 4.8 collective-permute-start.1
  107.2 4.3 gather_fusion.34
  111.4 4.2 gather_fusion.33
  119.0 4.5 collective-permute-start.3
  132.1 4.9 all-to-all-start
  140.1 45.9 %all-to-all-done = f32[8,64,1024]{2,0,1:T(8,128)S(1)} async-done(((f32[8,64,1024]{2,0,1:T(8,128)}), f32[8,64,1024]{2,0,1:T(8,128)S(1)}, u32[]{:S(2)}, u32[]{:S(2)}) %all-to-all-start) | async-done | bytes 2097184 | tf_op jit(solution)/shard_map/all_to_all | solution.py:117
  193.2 124.2 %all-reduce.11.cloned.1.call-done = f32[64,512]{0,1:T(8,128)} async-done(((f32[64,512]{0,1:T(8,128)}), f32[64,512]{0,1:T(8,128)}) %all-reduce.11.cloned.1.call-update) | async-done | bytes 131088 | tf_op jit(solution)/shard_map/psum | solution.py:135
  324.9 5.6 convolution_add_fusion.17
  330.4 5.6 convolution_add_fusion.16
  336.0 5.7 fusion.292
  341.7 4.0 copy.34
  350.1 123.9 %all-reduce.13.cloned.1.call-done = f32[64,512]{0,1:T(8,128)} async-done(((f32[64,512]{0,1:T(8,128)}), f32[64,512]{0,1:T(8,128)}) %all-reduce.13.cloned.1.call-update) | async-done | bytes 131088 | tf_op jit(solution)/shard_map/psum | solution.py:135
  481.4 5.6 convolution_add_fusion.14
  487.0 5.6 convolution_add_fusion.13
  492.6 5.7 fusion.295
  506.7 123.9 %all-reduce.15.cloned.1.call-done = f32[64,512]{0,1:T(8,128)} async-done(((f32[64,512]{0,1:T(8,128)}), f32[64,512]{0,1:T(8,128)}) %all-reduce.15.cloned.1.call-update) | async-done | bytes 131088 | tf_op jit(solution)/shard_map/psum | solution.py:135
  638.0 5.6 convolution_add_fusion.11
  643.6 5.6 convolution_add_fusion.10
  649.2 5.6 fusion.298
  662.2 123.7 %all-reduce.17.cloned.1.call-done = f32[64,512]{0,1:T(8,128)} async-done(((f32[64,512]{0,1:T(8,128)}), f32[64,512]{0,1:T(8,128)}) %all-reduce.17.cloned.1.call-update) | async-done | bytes 131088 | tf_op jit(solution)/shard_map/psum | solution.py:135
  793.3 5.6 convolution_add_fusion.8
  798.9 5.6 convolution_add_fusion.7
  804.4 5.7 fusion.301
  818.5 123.9 %all-reduce.19.cloned.1.call-done = f32[64,512]{0,1:T(8,128)} async-done(((f32[64,512]{0,1:T(8,128)}), f32[64,512]{0,1:T(8,128)}) %all-reduce.19.cloned.1.call-update) | async-done | bytes 131088 | tf_op jit(solution)/shard_map/psum | solution.py:135
  949.9 5.6 convolution_add_fusion.5
  955.5 5.6 convolution_add_fusion.4
  961.0 5.7 fusion.304
  975.2 124.1 %all-reduce.21.cloned.1.call-done = f32[64,512]{0,1:T(8,128)} async-done(((f32[64,512]{0,1:T(8,128)}), f32[64,512]{0,1:T(8,128)}) %all-reduce.21.cloned.1.call-update) | async-done | bytes 131088 | tf_op jit(solution)/shard_map/psum | solution.py:135
  1106.9 5.6 convolution_add_fusion.2
  1112.5 5.6 convolution_add_fusion.1
  1118.1 5.7 fusion.72
  1126.6 52.4 %all_to_all.33 = f32[64,8,1024]{2,1,0:T(8,128)S(1)} all-to-all(f32[64,8,1024]{2,1,0:T(8,128)S(1)} %bitcast.36), channel_id=1, replica_groups=mesh['member'=8,'state'=4] {'member'}, dimensions={0} | all-to-all | bytes 4194304 | tf_op jit(solution)/shard_map/all_to_all | solution.py:151
  (221 shorter events, 202.9 us)
Async XLA Ops:
  6.5 11.9 copy-start
  9.4 106.3 %collective-permute-start.1 = (f32[8,1,1024]{2,0,1:T(8,128)S(1)}, f32[8,1,1024]{2,0,1:T(8,128)S(1)}, u32[]{:S(2)}, u32[]{:S(2)}) collective-permute-start(f32[8,1,1024]{2,0,1:T(8,128)S(1)} %get-tuple-element.57), channel_id=1, source_target_pairs={{0,1},{1,2},{2,3},{4,5},{5,6},{6,7},{8,9},{9,10},{10,11},{12,13},{... | collective-permute-start | bytes 98312 | tf_op jit(solution)/shard_map/ppermute | solution.py:18
  14.2 101.4 %collective-permute-start = (f32[8,1,1024]{2,0,1:T(8,128)S(1)}, f32[8,1,1024]{2,0,1:T(8,128)S(1)}, u32[]{:S(2)}, u32[]{:S(2)}) collective-permute-start(f32[8,1,1024]{2,0,1:T(8,128)S(1)} %get-tuple-element.56), channel_id=1, source_target_pairs={{1,0},{2,1},{3,2},{5,4},{6,5},{7,6},{9,8},{10,9},{11,10},{13,12},{... | collective-permute-start | bytes 98312 | tf_op jit(solution)/shard_map/ppermute | solution.py:19
  18.3 6.5 copy-start.2
  18.4 12.8 %copy-start.3 = (s32[3072]{0:T(1024)S(1)}, s32[3072]{0:T(1024)}, u32[]{:S(2)}) copy-start(s32[3072]{0:T(1024)} %param.19) | copy-start | bytes 36868
  50.1 12.9 %copy-start.4 = (f32[3072]{0:T(1024)S(1)}, f32[3072]{0:T(1024)}, u32[]{:S(2)}) copy-start(f32[3072]{0:T(1024)} %param.16) | copy-start | bytes 36868
  56.5 12.9 %copy-start.5 = (f32[3072]{0:T(1024)S(1)}, f32[3072]{0:T(1024)}, u32[]{:S(2)}) copy-start(f32[3072]{0:T(1024)} %param.17) | copy-start | bytes 36868
  62.8 74.2 %copy-start.15 = (pred[512]{0:T(512)(128)(4,1)}, pred[512]{0:T(512)(128)(4,1)S(1)}, u32[]{:S(2)}) copy-start(pred[512]{0:T(512)(128)(4,1)S(1)} %get-tuple-element.8) | copy-start | bytes 1540
  100.8 14.8 %copy-start.10 = (f32[64,1024]{1,0:T(8,128)S(1)}, f32[64,1024]{1,0:T(8,128)}, u32[]{:S(2)}) copy-start(f32[64,1024]{1,0:T(8,128)} %param.15) | copy-start | bytes 786436
  119.0 7.1 collective-permute-start.3
  123.6 6.2 collective-permute-start.2
  132.1 53.9 %all-to-all-start = ((f32[8,64,1024]{2,0,1:T(8,128)}), f32[8,64,1024]{2,0,1:T(8,128)S(1)}, u32[]{:S(2)}, u32[]{:S(2)}) async-start(f32[8,64,1024]{2,0,1:T(8,128)} %fusion.82), calls=%async_computation | async-start | bytes 4194304 | tf_op jit(solution)/shard_map/all_to_all | solution.py:117
  137.0 180.5 %all-reduce.11.cloned.1.call-start = ((), (), s32[]{:S(2)}) async-start(), calls=%async_computation.2 | async-start | bytes 524288 | tf_op jit(solution)/shard_map/psum | solution.py:135
  192.9 281.1 %all-reduce.13.cloned.1.call-start = ((), (), s32[]{:S(2)}) async-start(), calls=%async_computation.3 | async-start | bytes 524288 | tf_op jit(solution)/shard_map/psum | solution.py:135
  341.7 135.8 %copy-start.6 = (f32[64,8192]{1,0:T(8,128)S(1)}, f32[64,8192]{1,0:T(8,128)}, u32[]{:S(2)}) copy-start(f32[64,8192]{1,0:T(8,128)} %get-tuple-element.201) | copy-start | bytes 6291460
  349.8 280.7 %all-reduce.15.cloned.1.call-start = ((), (), s32[]{:S(2)}) async-start(), calls=%async_computation.4 | async-start | bytes 524288 | tf_op jit(solution)/shard_map/psum | solution.py:135
  498.3 135.8 %copy-start.7 = (f32[64,8192]{1,0:T(8,128)S(1)}, f32[64,8192]{1,0:T(8,128)}, u32[]{:S(2)}) copy-start(f32[64,8192]{1,0:T(8,128)} %get-tuple-element.203) | copy-start | bytes 6291460
  506.4 279.5 %all-reduce.17.cloned.1.call-start = ((), (), s32[]{:S(2)}) async-start(), calls=%async_computation.5 | async-start | bytes 524288 | tf_op jit(solution)/shard_map/psum | solution.py:135
  661.7 280.7 %all-reduce.19.cloned.1.call-start = ((), (), s32[]{:S(2)}) async-start(), calls=%async_computation.6 | async-start | bytes 524288 | tf_op jit(solution)/shard_map/psum | solution.py:135
  810.2 135.8 %copy-start.8 = (f32[64,8192]{1,0:T(8,128)S(1)}, f32[64,8192]{1,0:T(8,128)}, u32[]{:S(2)}) copy-start(f32[64,8192]{1,0:T(8,128)} %get-tuple-element.207) | copy-start | bytes 6291460
  818.3 281.0 %all-reduce.21.cloned.1.call-start = ((), (), s32[]{:S(2)}) async-start(), calls=%async_computation.7 | async-start | bytes 524288 | tf_op jit(solution)/shard_map/psum | solution.py:135
  966.8 7.5 copy-start.17
  966.8 7.5 copy-start.18
  966.8 134.8 %copy-start.13 = (f32[512]{0:T(512)S(1)}, f32[512]{0:T(512)}, u32[]{:S(2)}) copy-start(f32[512]{0:T(512)} %gather_fusion.34) | copy-start | bytes 6148
  966.8 134.8 %copy-start.14 = (f32[512]{0:T(512)S(1)}, f32[512]{0:T(512)}, u32[]{:S(2)}) copy-start(f32[512]{0:T(512)} %gather_fusion.33) | copy-start | bytes 6148
  966.8 134.8 %copy-start.16 = (pred[512]{0:T(512)(128)(4,1)S(1)}, pred[512]{0:T(512)(128)(4,1)}, u32[]{:S(2)}) copy-start(pred[512]{0:T(512)(128)(4,1)} %copy-done.15) | copy-start | bytes 1540
  966.8 136.1 %copy-start.9 = (f32[64,8192]{1,0:T(8,128)S(1)}, f32[64,8192]{1,0:T(8,128)}, u32[]{:S(2)}) copy-start(f32[64,8192]{1,0:T(8,128)} %get-tuple-element.209) | copy-start | bytes 6291460
  966.8 136.1 %copy-start.25 = (s32[128]{0:T(128)S(1)}, s32[128]{0:T(128)}, u32[]{:S(2)}) copy-start(s32[128]{0:T(128)} %get-tuple-element.101) | copy-start | bytes 1540
  966.8 136.1 %copy-start.26 = (s32[128]{0:T(128)S(1)}, s32[128]{0:T(128)}, u32[]{:S(2)}) copy-start(s32[128]{0:T(128)} %get-tuple-element.237) | copy-start | bytes 1540
  966.8 136.1 %copy-start.30 = (f32[128]{0:T(128)S(1)}, f32[128]{0:T(128)}, u32[]{:S(2)}) copy-start(f32[128]{0:T(128)} %get-tuple-element.109) | copy-start | bytes 1540
  1112.5 5.6 copy-start.19
  1126.6 53.9 %copy-start.1 = (s32[3072]{0:T(1024)S(1)}, s32[3072]{0:T(1024)}, u32[]{:S(2)}) copy-start(s32[3072]{0:T(1024)} %param.20) | copy-start | bytes 36868
  (10 other events, 47.9 us)
Sparse Core Ops, SparseCore 0:
  193.0 124.3 all-reduce.10
  350.0 123.9 all-reduce.12
  506.5 123.9 all-reduce.14
  661.9 123.9 all-reduce.16
  818.4 123.9 all-reduce.18
  975.3 123.9 all-reduce.20
where the time goes:
time: 1190 us
  waiting for transfers between devices  793 us (67%)
  local copies, waits for them, and re-layouts  149 us (13%)
  matrix products  125 us (11%)
  blocking collectives  52.4 us (4%)
  other arithmetic  34.9 us (3%)
  starting transfers between devices  18.5 us (2%)
  between operations  14.9 us (1%)
    psum x6, waiting for transfers between devices, on_device(): prior_values = lax.psum(local_values, ('member', 'state'))  744 us
    dot_general x24, matrix products, linear_gain_fit(): jnp.dot(increment[:, lower_end:upper_end], gain_tile, preferred_element_t...  125 us
    all_to_all x1, blocking collectives, on_device(): lax.all_to_all(result, 'member', split_axis=0, concat_axis=1, tiled=True)  52.4 us
    all_to_all x1, waiting for transfers between devices, on_device(): lax.all_to_all(realization_vectors, 'member', split_axis=1, concat_axis=0...  45.9 us
  transfers between devices with their start and end apart: 11, of which 8 were waited for; matrix products, arithmetic and copies ran while one was open for 9% of the time, Pallas kernels for 0%

commit v1 on v0

--- a/solution.py
+++ b/solution.py
@@ -132,7 +132,7 @@
         local_values = pick_values(
             cell_values, block_rows, block_cols, first_row, tile_rows, col_count
         )
-        prior_values = lax.psum(local_values, ("member", "state"))
+        prior_values = jnp.sum(lax.all_gather(local_values, ("member", "state")), axis=0)
         anomaly, increment, inverse = increments(
             prior_values, jnp.take(observations, chosen), jnp.take(obs_variance, chosen)
         )

time: 1190 us -> 726 us (0.61)
  waiting for transfers between devices: 793 us -> 323 us
    psum x6 -> x0, waiting for transfers between devices: 744 us -> none  [on_device(): prior_values = lax.psum(local_values, ('member', 'state'))]
    all_gather x0 -> x6, waiting for transfers between devices: none -> 292 us  [on_device(): lax.all_gather(local_values, ('member', 'state'))]
    all_to_all x1, waiting for transfers between devices: 45.9 us -> 23.6 us  [on_device(): lax.all_to_all(realization_vectors, 'member', split_axis=1, concat_axis=0...]
    reduce_sum x0 -> x6, other arithmetic: none -> 15.8 us  [on_device(): jnp.sum(lax.all_gather(local_values, ('member', 'state')), axis=0)]
  transfers between devices with their start and end apart: 11 -> 11, of which waited for: 8 -> 9; matrix products, arithmetic and copies ran while one was open for 9% -> 14% of each run, Pallas kernels for 0% -> 0%
where the time goes in v1:
time: 726 us; the launch traced here: 717 us
  waiting for transfers between devices  323 us (44%)
  local copies, waits for them, and re-layouts  149 us (21%)
  matrix products  124 us (17%)
  blocking collectives  52 us (7%)
  other arithmetic  36.6 us (5%)
  starting transfers between devices  17.1 us (2%)
  between operations  14.7 us (2%)
    all_gather x6, waiting for transfers between devices, on_device(): lax.all_gather(local_values, ('member', 'state'))  292 us
    dot_general x24, matrix products, linear_gain_fit(): jnp.dot(increment[:, lower_end:upper_end], gain_tile, preferred_element_t...  124 us
    all_to_all x1, blocking collectives, on_device(): lax.all_to_all(result, 'member', split_axis=0, concat_axis=1, tiled=True)  52 us
    all_to_all x1, waiting for transfers between devices, on_device(): lax.all_to_all(realization_vectors, 'member', split_axis=1, concat_axis=0...  23.6 us
    gather x6, local copies, waits for them, and re-layouts, on_device(): jnp.take(observations, chosen)  20 us
    gather x6, local copies, waits for them, and re-layouts, pick_values(): jnp.take(cell_values, local_index, axis=1)  19.3 us
    gather x6, local copies, waits for them, and re-layouts, on_device(): jnp.take(obs_variance, chosen)  19.2 us
    gather x6, local copies, waits for them, and re-layouts, on_device(): block_rows = jnp.take(obs_row, chosen)  18.9 us
  transfers between devices with their start and end apart: 11, of which 9 were waited for; matrix products, arithmetic and copies ran while one was open for 14% of the time, Pallas kernels for 0%

profile of v1, /device:TPU:0, one launch (start us, length us, event | category | flops | bytes accessed | tf_op | source)
XLA Modules:
  0.0 716.9 jit_solution(11982546438807816886)
XLA Ops:
  9.4 4.8 collective-permute-start.1
  21.3 4.3 collective-permute-start.3
  33.8 5.0 all-to-all-start
  64.3 23.6 %all-to-all-done = f32[8,64,1024]{2,0,1:T(8,128)S(1)} async-done(((f32[8,64,1024]{2,0,1:T(8,128)}), f32[8,64,1024]{2,0,1:T(8,128)S(1)}, u32[]{:S(2)}, u32[]{:S(2)}) %all-to-all-start) | async-done | bytes 2097184 | tf_op jit(solution)/shard_map/all_to_all | solution.py:117
  108.0 46.9 %all-gather.13.cloned.1.call-done = f32[2048,512]{1,0:T(8,128)} async-done(((f32[64,512]{1,0:T(8,128)}), f32[2048,512]{1,0:T(8,128)}) %all-gather.13.cloned.1.call-update) | async-done | bytes 4194320 | tf_op jit(solution)/shard_map/all_gather | solution.py:135
  160.1 3.9 fusion.93
  164.0 5.6 convolution_add_fusion.17
  169.6 5.6 convolution_add_fusion.16
  175.2 5.7 fusion.292
  208.3 41.3 %all-gather.15.cloned.1.call-done = f32[2048,512]{1,0:T(8,128)} async-done(((f32[64,512]{1,0:T(8,128)}), f32[2048,512]{1,0:T(8,128)}) %all-gather.15.cloned.1.call-update) | async-done | bytes 4194320 | tf_op jit(solution)/shard_map/all_gather | solution.py:135
  258.8 5.6 convolution_add_fusion.14
  264.4 5.6 convolution_add_fusion.13
  270.0 5.7 fusion.295
  290.2 54.1 %all-gather.17.cloned.1.call-done = f32[2048,512]{1,0:T(8,128)} async-done(((f32[64,512]{1,0:T(8,128)}), f32[2048,512]{1,0:T(8,128)}) %all-gather.17.cloned.1.call-update) | async-done | bytes 4194320 | tf_op jit(solution)/shard_map/all_gather | solution.py:135
  349.7 3.9 fusion.91
  353.6 5.6 convolution_add_fusion.11
  359.2 5.6 convolution_add_fusion.10
  364.8 5.6 fusion.298
  396.9 41.3 %all-gather.19.cloned.1.call-done = f32[2048,512]{1,0:T(8,128)} async-done(((f32[64,512]{1,0:T(8,128)}), f32[2048,512]{1,0:T(8,128)}) %all-gather.19.cloned.1.call-update) | async-done | bytes 4194320 | tf_op jit(solution)/shard_map/all_gather | solution.py:135
  447.2 5.6 convolution_add_fusion.8
  452.8 5.6 convolution_add_fusion.7
  458.4 5.7 fusion.301
  478.6 54.2 %all-gather.21.cloned.1.call-done = f32[2048,512]{1,0:T(8,128)} async-done(((f32[64,512]{1,0:T(8,128)}), f32[2048,512]{1,0:T(8,128)}) %all-gather.21.cloned.1.call-update) | async-done | bytes 4194320 | tf_op jit(solution)/shard_map/all_gather | solution.py:135
  542.0 5.6 convolution_add_fusion.5
  547.6 5.6 convolution_add_fusion.4
  553.2 5.7 fusion.304
  573.4 54.2 %all-gather.23.cloned.1.call-done = f32[2048,512]{1,0:T(8,128)} async-done(((f32[64,512]{1,0:T(8,128)}), f32[2048,512]{1,0:T(8,128)}) %all-gather.23.cloned.1.call-update) | async-done | bytes 4194320 | tf_op jit(solution)/shard_map/all_gather | solution.py:135
  632.9 3.9 fusion.88
  636.8 5.6 convolution_add_fusion.2
  642.4 5.6 convolution_add_fusion.1
  647.9 5.6 fusion.72
  656.4 52.0 %all_to_all.33 = f32[64,8,1024]{2,1,0:T(8,128)S(1)} all-to-all(f32[64,8,1024]{2,1,0:T(8,128)S(1)} %bitcast.48), channel_id=1, replica_groups=mesh['member'=8,'state'=4] {'member'}, dimensions={0} | all-to-all | bytes 4194304 | tf_op jit(solution)/shard_map/all_to_all | solution.py:151
  (193 shorter events, 207.9 us)
Async XLA Ops:
  6.5 32.3 %copy-start = (s32[3072]{0:T(1024)S(1)}, s32[3072]{0:T(1024)}, u32[]{:S(2)}) copy-start(s32[3072]{0:T(1024)} %param.20) | copy-start | bytes 36868
  9.4 7.1 collective-permute-start.1
  14.2 6.0 copy-start.10
  14.2 5.9 collective-permute-start
  21.3 6.4 collective-permute-start.3
  25.6 5.8 collective-permute-start.2
  33.8 5.1 copy-start.11
  33.8 54.1 %all-to-all-start = ((f32[8,64,1024]{2,0,1:T(8,128)}), f32[8,64,1024]{2,0,1:T(8,128)S(1)}, u32[]{:S(2)}, u32[]{:S(2)}) async-start(f32[8,64,1024]{2,0,1:T(8,128)} %fusion.82), calls=%async_computation | async-start | bytes 4194304 | tf_op jit(solution)/shard_map/all_to_all | solution.py:117
  38.8 116.2 %all-gather.13.cloned.1.call-start = ((), (), s32[]{:S(2)}) async-start(), calls=%async_computation.2 | async-start | bytes 4325376 | tf_op jit(solution)/shard_map/all_gather | solution.py:135
  45.2 12.7 %copy-start.2 = (s32[3072]{0:T(1024)S(1)}, s32[3072]{0:T(1024)}, u32[]{:S(2)}) copy-start(s32[3072]{0:T(1024)} %param.18) | copy-start | bytes 36868
  48.4 12.7 %copy-start.3 = (s32[3072]{0:T(1024)S(1)}, s32[3072]{0:T(1024)}, u32[]{:S(2)}) copy-start(s32[3072]{0:T(1024)} %param.19) | copy-start | bytes 36868
  90.5 10.6 %copy-start.4 = (f32[3072]{0:T(1024)S(1)}, f32[3072]{0:T(1024)}, u32[]{:S(2)}) copy-start(f32[3072]{0:T(1024)} %param.16) | copy-start | bytes 36868
  90.5 13.8 %copy-start.5 = (f32[3072]{0:T(1024)S(1)}, f32[3072]{0:T(1024)}, u32[]{:S(2)}) copy-start(f32[3072]{0:T(1024)} %param.17) | copy-start | bytes 36868
  94.8 154.8 %all-gather.15.cloned.1.call-start = ((), (), s32[]{:S(2)}) async-start(), calls=%async_computation.3 | async-start | bytes 4325376 | tf_op jit(solution)/shard_map/all_gather | solution.py:135
  188.9 155.5 %all-gather.17.cloned.1.call-start = ((), (), s32[]{:S(2)}) async-start(), calls=%async_computation.4 | async-start | bytes 4325376 | tf_op jit(solution)/shard_map/all_gather | solution.py:135
  249.6 5.3 copy-start.6
  283.6 154.5 %all-gather.19.cloned.1.call-start = ((), (), s32[]{:S(2)}) async-start(), calls=%async_computation.5 | async-start | bytes 4325376 | tf_op jit(solution)/shard_map/all_gather | solution.py:135
  344.4 5.3 copy-start.8
  377.4 155.4 %all-gather.21.cloned.1.call-start = ((), (), s32[]{:S(2)}) async-start(), calls=%async_computation.6 | async-start | bytes 4325376 | tf_op jit(solution)/shard_map/all_gather | solution.py:135
  472.0 155.5 %all-gather.23.cloned.1.call-start = ((), (), s32[]{:S(2)}) async-start(), calls=%async_computation.7 | async-start | bytes 4325376 | tf_op jit(solution)/shard_map/all_gather | solution.py:135
  532.8 5.3 copy-start.7
  627.6 5.3 copy-start.9
  656.3 53.5 %copy-start.1 = (s32[3072]{0:T(1024)S(1)}, s32[3072]{0:T(1024)}, u32[]{:S(2)}) copy-start(s32[3072]{0:T(1024)} %param.20) | copy-start | bytes 36868
Sparse Core Ops, SparseCore 0:
  94.9 59.9 all-gather.12
  189.0 60.5 all-gather.14
  283.8 60.5 all-gather.16
  377.5 60.5 all-gather.18
  472.2 60.5 all-gather.20
  566.9 60.5 all-gather.22
